TPU v7x, 32 devices: a whole 2x2x4 slice. The times are simulated.
32 devices in a mesh: groups: 2 (over y), dp: 16 (over z, x, core).
Axes of the slice: x: 2, y: 2, z: 4, core: 2. Of those that a mesh axis runs over, the one named last changes fastest.
Arguments:
- hidden_in: bfloat16 [2, 4096, 14336], P(None, ('groups', 'dp')), parts along dimension 1, may hold values from -6 to 6
- out_grad: bfloat16 [2, 4096, 4096], P(None, ('groups', 'dp')), parts along dimension 1, may hold values from -6 to 6
- proj_hidden: bfloat16 [2, 14336, 64], P(None, 'dp'), may hold values from -0.046875 to 0.046875
- proj_out: bfloat16 [2, 4096, 64], replicated, may hold values from -0.09375 to 0.09375
- lengths: int32 [32], P(('groups', 'dp')), parts along dimension 0, may hold values from 64 to 128
- query_sketch: bfloat16 [512, 8192], P(('groups', 'dp')), parts along dimension 0, may hold values from -6 to 6
Outputs:
- scores: float32 [512, 16], P(('groups', 'dp')), parts along dimension 0
There are 2 independent parts, one for each index of `groups`. A program takes and returns all parts, laid end to end along the dimension named above; an argument that names none is the same for every part. Nothing has to cross between parts.
All inputs are finite; a program needn't handle non-finite values.
Results may differ from a plain program's by a relative error of at most 0.0029.
Values may be sent and summed in bfloat16 or wider, within the bound.
A program may use at most 64 MiB of HBM per device.

v0:
```python
import math

import jax
import jax.numpy as jnp
from jax import lax
from jax.sharding import PartitionSpec as P

LEN = 128


def on_device(hidden_in, out_grad, proj_hidden, proj_out, lengths, query_sketch):
    layer_count = hidden_in.shape[0]
    rank_size = proj_out.shape[2]
    tok_rows = out_grad.shape[1]
    seq_count = lengths.shape[0]
    position = jnp.arange(tok_rows, dtype=jnp.int32)
    length_limit = jnp.repeat(lengths, LEN)
    kept_mask = (position % LEN < length_limit).astype(jnp.float32)
    inputs = jnp.einsum(
        "lth,lhr->ltr",
        hidden_in,
        lax.all_gather(proj_hidden, "dp", axis=1, tiled=True),
        preferred_element_type=jnp.float32,
    )
    sketches = []
    for layer in range(layer_count):
        projected_out = jnp.dot(
            out_grad[layer], proj_out[layer], preferred_element_type=jnp.float32
        )
        projected_out = projected_out * kept_mask[:, None]
        sketch = jnp.einsum(
            "epa,epb->eab",
            projected_out.reshape(seq_count, LEN, rank_size),
            inputs[layer].reshape(seq_count, LEN, rank_size),
            precision=lax.Precision.HIGHEST,
        )
        sketches.append(sketch * (1.0 / math.sqrt(LEN)))
    stacked = jnp.stack(sketches, axis=1).reshape(seq_count, layer_count * rank_size * rank_size)
    stacked = stacked.astype(jnp.bfloat16)
    score_scale = 1.0 / math.sqrt(layer_count * rank_size * rank_size)
    product = lax.dot_general(
        query_sketch,
        lax.all_gather(stacked, "dp", axis=0, tiled=True),
        (((1,), (1,)), ((), ())),
        preferred_element_type=jnp.float32,
    )
    return product * score_scale


def solution(mesh):
    return jax.shard_map(
        on_device,
        mesh=mesh,
        in_specs=(
            P(None, ("groups", "dp"), None),
            P(None, ("groups", "dp"), None),
            P(None, "dp", None),
            P(),
            P(("groups", "dp")),
            P(("groups", "dp"), None),
        ),
        out_specs=P(("groups", "dp"), None),
        check_vma=False,
    )
```

profile of v0, /device:TPU:0, one launch (start us, length us, event | category | flops | bytes accessed | tf_op | source)
XLA Modules:
  0.0 96.0 jit_solution(13855180391033439384)
XLA Ops:
  6.5 0.0 copy-start
  6.5 0.0 all-gather.3.cloned.1.call-start
  6.5 0.7 all-gather.3.cloned.1.call-update
  7.9 1.8 %convolution_multiply_fusion.1 = f32[128,64]{0,1:T(8,128)S(1)} fusion(bf16[2,128,4096]{2,1,0:T(8,128)(2,1)} %param.7, bf16[2,4096,64]{1,2,0:T(8,128)(2,1)} %param.9, f32[128]{0:T(128)S(1)} %compare_convert_fusion), kind=kOutput, calls=%fused_computation.1 | convolution fusion | flops 67117056 | bytes 1606144 | tf_op jit(solution)/shard_map/dot_general | solution.py:27
  9.8 1.8 %convolution_multiply_fusion.3 = f32[128,64]{0,1:T(8,128)S(1)} fusion(bf16[2,128,4096]{2,1,0:T(8,128)(2,1)} %param.7, bf16[2,4096,64]{1,2,0:T(8,128)(2,1)} %param.9, f32[128]{0:T(128)S(1)} %compare_convert_fusion), kind=kOutput, calls=%fused_computation.3 | convolution fusion | flops 67117056 | bytes 1606144 | tf_op jit(solution)/shard_map/dot_general | solution.py:27
  11.6 48.7 %all-gather.3.cloned.1.call-done = bf16[2,14336,64]{1,2,0:T(8,128)(2,1)} async-done(((bf16[2,896,64]{1,2,0:T(8,128)(2,1)}), bf16[2,14336,64]{1,2,0:T(8,128)(2,1)}) %all-gather.3.cloned.1.call-update) | async-done | bytes 3670032 | tf_op jit(solution)/shard_map/all_gather | solution.py:22
  60.4 6.8 %fusion.15 = f32[2,128,64]{1,2,0:T(8,128)S(1)} fusion(bf16[2,128,14336]{2,1,0:T(8,128)(2,1)} %param.6, bf16[2,14336,64]{1,2,0:T(8,128)(2,1)} %all-gather.3.cloned.1.call-done), kind=kOutput, calls=%fused_computation.25 | convolution fusion | flops 469762048 | bytes 11075584 | tf_op jit(solution)/shard_map/lth,lhr->ltr/dot_general | solution.py:19
  67.1 0.2 fusion.2
  67.3 0.2 fusion.3
  67.5 0.1 reshape.50
  67.6 20.5 %all-gather = bf16[16,1,8192]{2,1,0:T(2,128)(2,1)S(1)} all-gather(bf16[1,1,8192]{2,1,0:T(2,128)(2,1)S(1)} %reshape.50), channel_id=1, replica_groups=mesh['groups'=2,'dp'=16] {'dp'}, dimensions={0}, use_global_device_ids=true | all-gather | bytes 278528 | tf_op jit(solution)/shard_map/all_gather | solution.py:43
  88.1 0.0 copy-done
  88.1 0.4 fusion.4
  88.5 0.7 copy.10
  (2 shorter events, 0.0 us)
Async XLA Ops:
  6.5 81.5 %copy-start = (bf16[16,8192]{1,0:T(8,128)(2,1)S(1)}, bf16[16,8192]{1,0:T(8,128)(2,1)}, u32[]{:S(2)}) copy-start(bf16[16,8192]{1,0:T(8,128)(2,1)} %param.11) | copy-start | bytes 786436
  6.5 53.8 %all-gather.3.cloned.1.call-start = ((), (), s32[]{:S(2)}) async-start(), calls=%async_computation | async-start | bytes 3899392 | tf_op jit(solution)/shard_map/all_gather | solution.py:22
Sparse Core Ops, SparseCore 0:
  9.5 50.7 all-gather.2
where the time goes:
time: 96.2 us; the launch traced here: 96 us
  waiting for transfers between devices  49.5 us (51%)
  blocking collectives  20.5 us (21%)
  between operations  14.1 us (15%)
  matrix products  11.2 us (12%)
    all_gather x1, waiting for transfers between devices, on_device(): lax.all_gather(proj_hidden, 'dp', axis=1, tiled=True)  48.7 us
    all_gather x1, blocking collectives, on_device(): lax.all_gather(stacked, 'dp', axis=0, tiled=True)  20.5 us
    dot_general x1, matrix products, on_device(): jnp.einsum('lth,lhr->ltr', hidden_in, lax.all_gather(proj_hidden, 'dp', a...  6.77 us
    dot_general x2, matrix products, on_device(): jnp.dot(out_grad[layer], proj_out[layer], preferred_element_type=jnp.floa...  3.68 us
  transfers between devices with their start and end apart: 1, of which 1 were waited for; matrix products, arithmetic and copies ran while one was open for 4% of the time, Pallas kernels for 0%

commit v1 on v0

--- a/solution.py
+++ b/solution.py
@@ -1,14 +1,19 @@
+import functools
 import math
 
 import jax
 import jax.numpy as jnp
 from jax import lax
+from jax.experimental import pallas as pl
+from jax.experimental.pallas import tpu as pltpu
 from jax.sharding import PartitionSpec as P
 
 LEN = 128
-
-
-def on_device(hidden_in, out_grad, proj_hidden, proj_out, lengths, query_sketch):
+MESH = pl.DeviceIdType.MESH
+ROWS_BY_ROWS = (((1,), (1,)), ((), ()))
+
+
+def plain(hidden_in, out_grad, proj_hidden, proj_out, lengths, query_sketch):
     layer_count = hidden_in.shape[0]
     rank_size = proj_out.shape[2]
     tok_rows = out_grad.shape[1]
@@ -47,7 +52,242 @@
     return product * score_scale
 
 
+def fused_kernel(
+    n, len_ref, hid_ref, grad_ref, fac_ref, pout_ref, query_ref, out_ref,
+    hid, grad, pout, query, held, turned, sketches, spread,
+    load_sem, ring_send, ring_recv, pair_send, pair_recv, sk_send, sk_recv,
+):
+    layers, rank, depth = fac_ref.shape
+    chips = n // 2
+    half = chips // 2
+    row_half = rank // 2
+    me = lax.axis_index("dp")
+    core = me % 2
+    chip = me // 2
+    odd = chip % 2
+    place = (1 - odd) * (chip // 2) + odd * (chips - 1 - chip // 2)
+
+    def device_at(spot, which):
+        spot = lax.rem(spot + 2 * chips, chips)
+        upper = spot // half
+        return 2 * ((1 - upper) * 2 * spot + upper * (2 * (chips - 1 - spot) + 1)) + which
+
+    up = device_at(place + 1, core)
+    down = device_at(place - 1, core)
+    pair = me + 1 - 2 * core
+
+    loads = []
+
+    def load(src, dst):
+        copy = pltpu.make_async_copy(src, dst, load_sem.at[len(loads)])
+        copy.start()
+        loads.append(copy)
+        return copy
+
+    barrier = pltpu.get_barrier_semaphore()
+    for step in range(1, n):
+        pl.semaphore_signal(
+            barrier, inc=1, device_id={"dp": lax.rem(me + step, n)}, device_id_type=MESH
+        )
+    load_grad = load(grad_ref, grad)
+    load_pout = load(pout_ref, pout)
+    load_own = load(fac_ref, held.at[:, 0, 0])
+    load_hid = [load(hid_ref.at[layer], hid.at[layer]) for layer in range(layers)]
+    load_query = load(query_ref, query)
+    pl.semaphore_wait(barrier, n - 1)
+
+    sent = []
+
+    def send(src, dst, send_sem, recv_sem, device):
+        copy = pltpu.make_async_remote_copy(
+            src_ref=src, dst_ref=dst, send_sem=send_sem, recv_sem=recv_sem,
+            device_id={"dp": device}, device_id_type=MESH,
+        )
+        copy.start()
+        sent.append(copy)
+        return copy
+
+    def rows_of(slot):
+        if slot == chips:
+            return half, pl.ds(row_half, rank - row_half)
+        if slot == half:
+            return half, pl.ds(0, row_half)
+        return slot, pl.ds(0, rank)
+
+    def ring(layer, src, slot, device):
+        where, rows = rows_of(slot)
+        return send(
+            src.at[rows], held.at[layer, 0, where, rows],
+            ring_send.at[layer, slot], ring_recv.at[layer, slot], device,
+        )
+
+    def across(layer, slot):
+        where, rows = rows_of(slot)
+        return send(
+            held.at[layer, 0, where, rows], held.at[layer, 1, where, rows],
+            pair_send.at[layer, slot], pair_recv.at[layer, slot], pair,
+        )
+
+    def arrived(layer, bank, slot):
+        where, rows = rows_of(slot)
+        ref = held.at[layer, bank, where, rows]
+        sems = (pair_send, pair_recv) if bank else (ring_send, ring_recv)
+        pltpu.make_async_remote_copy(
+            src_ref=ref, dst_ref=ref, send_sem=sems[0].at[layer, slot], recv_sem=sems[1].at[layer, slot],
+            device_id={"dp": pair}, device_id_type=MESH,
+        ).wait_recv()
+
+    for layer in range(layers):
+        ring(layer, fac_ref.at[layer], 1, up)
+        ring(layer, fac_ref.at[layer], chips - 1, down)
+    load_own.wait()
+    for layer in range(layers):
+        across(layer, 0)
+
+    load_grad.wait()
+    load_pout.wait()
+    count = len_ref[0]
+    kept = (lax.broadcasted_iota(jnp.int32, (rank, LEN), 1) < count).astype(jnp.float32)
+    left = []
+    for layer in range(layers):
+        turned[layer] = kept * lax.dot_general(
+            pout[layer], grad[layer], ROWS_BY_ROWS, preferred_element_type=jnp.float32
+        )
+        left.append(jnp.concatenate(
+            [turned[layer, pl.ds(0, rank // 2, stride=2), :], turned[layer, pl.ds(1, rank // 2, stride=2), :]],
+            axis=0,
+        ))
+
+    totals = [jnp.zeros((LEN, rank), jnp.float32) for _ in range(layers)]
+
+    def add(layer, bank, slot):
+        owner = device_at(place - slot, core if bank == 0 else 1 - core)
+        columns = pl.ds(pl.multiple_of(owner * depth, depth), depth)
+        totals[layer] += lax.dot_general(
+            hid[layer, :, columns], held[layer, bank, slot], ROWS_BY_ROWS, preferred_element_type=jnp.float32
+        )
+
+    def finish(layer):
+        sketch = lax.dot_general(
+            left[layer], totals[layer], (((1,), (0,)), ((), ())),
+            precision=lax.Precision.HIGHEST, preferred_element_type=jnp.float32,
+        ) * (1.0 / math.sqrt(LEN))
+        flat = jnp.concatenate([sketch[: rank // 2], sketch[rank // 2 :]], axis=1)
+        sketches[layer, me] = flat.astype(jnp.bfloat16)
+        for step in range(1, n):
+            send(
+                sketches.at[layer, me], sketches.at[layer, me],
+                sk_send.at[layer, step], sk_recv.at[layer, step], lax.rem(me + step, n),
+            )
+
+    for layer in range(layers):
+        load_hid[layer].wait()
+        add(layer, 0, 0)
+    for hop in range(1, half + 1):
+        for layer in range(layers):
+            if hop < half:
+                arrived(layer, 0, hop)
+                ring(layer, held.at[layer, 0, hop], hop + 1, up)
+                across(layer, hop)
+                arrived(layer, 0, chips - hop)
+                ring(layer, held.at[layer, 0, chips - hop], chips - hop - 1 if hop + 1 < half else chips, down)
+                across(layer, chips - hop)
+                add(layer, 0, hop)
+                add(layer, 0, chips - hop)
+            else:
+                arrived(layer, 0, half)
+                across(layer, half)
+                arrived(layer, 0, chips)
+                across(layer, chips)
+                add(layer, 0, half)
+            if hop == 1:
+                arrived(layer, 1, 0)
+                add(layer, 1, 0)
+            else:
+                for slot in (hop - 1, chips - hop + 1):
+                    arrived(layer, 1, slot)
+                    add(layer, 1, slot)
+            if hop == half:
+                arrived(layer, 1, half)
+                arrived(layer, 1, chips)
+                add(layer, 1, half)
+                finish(layer)
+
+    load_query.wait()
+    scores = jnp.zeros((query.shape[0], n), jnp.float32)
+    width = rank * rank
+    for layer in range(layers):
+        for step in range(1, n):
+            ref = sketches.at[layer, lax.rem(me + n - step, n)]
+            pltpu.make_async_remote_copy(
+                src_ref=ref, dst_ref=ref, send_sem=sk_send.at[layer, step], recv_sem=sk_recv.at[layer, step],
+                device_id={"dp": pair}, device_id_type=MESH,
+            ).wait_recv()
+        lines = width // 128
+        spread[...] = sketches[layer].astype(jnp.float32).reshape(n * lines, 128)
+        flat = jnp.concatenate(
+            [spread[pl.ds(line, n, stride=lines), :].astype(jnp.bfloat16) for line in range(lines)], axis=1
+        )
+        scores += lax.dot_general(
+            query[:, layer * width : (layer + 1) * width], flat, ROWS_BY_ROWS, preferred_element_type=jnp.float32
+        )
+    out_ref[...] = scores * (1.0 / math.sqrt(layers * width))
+    for copy in sent:
+        copy.wait_send()
+
+
+def fused(n, hidden_in, out_grad, proj_hidden, proj_out, lengths, query_sketch):
+    layers, tokens, hidden = hidden_in.shape
+    depth, rank = proj_hidden.shape[1:]
+    queries = query_sketch.shape[0]
+    lines = rank * rank // 128
+    slots = n // 2 + 1
+    dma = pltpu.SemaphoreType.DMA
+    return pl.pallas_call(
+        functools.partial(fused_kernel, n),
+        out_shape=jax.ShapeDtypeStruct((queries, n), jnp.float32),
+        in_specs=[pl.BlockSpec(memory_space=pltpu.SMEM)] + [pl.BlockSpec(memory_space=pl.ANY)] * 5,
+        out_specs=pl.BlockSpec(memory_space=pltpu.VMEM),
+        scratch_shapes=[
+            pltpu.VMEM((layers, tokens, hidden), jnp.bfloat16),
+            pltpu.VMEM(out_grad.shape, jnp.bfloat16),
+            pltpu.VMEM((layers, rank, proj_out.shape[1]), jnp.bfloat16),
+            pltpu.VMEM(query_sketch.shape, jnp.bfloat16),
+            pltpu.VMEM((layers, 2, n // 2, rank, depth), jnp.bfloat16),
+            pltpu.VMEM((layers, rank, LEN), jnp.float32),
+            pltpu.VMEM((layers, n, lines, 128), jnp.bfloat16),
+            pltpu.VMEM((n * lines, 128), jnp.float32),
+            dma((8,)),
+            dma((layers, slots)),
+            dma((layers, slots)),
+            dma((layers, slots)),
+            dma((layers, slots)),
+            dma((layers, n)),
+            dma((layers, n)),
+        ],
+        compiler_params=pltpu.CompilerParams(
+            collective_id=0, has_side_effects=True, vmem_limit_bytes=48 << 20
+        ),
+        cost_estimate=pl.CostEstimate(
+            flops=2 * layers * tokens * rank * (hidden + out_grad.shape[2]),
+            bytes_accessed=2 * layers * tokens * (hidden + out_grad.shape[2]),
+            transcendentals=0,
+        ),
+    )(
+        lengths, hidden_in, out_grad, jnp.swapaxes(proj_hidden, 1, 2), jnp.swapaxes(proj_out, 1, 2), query_sketch
+    )
+
+
 def solution(mesh):
+    n = mesh.shape["dp"]
+
+    def on_device(hidden_in, out_grad, proj_hidden, proj_out, lengths, query_sketch):
+        args = (hidden_in, out_grad, proj_hidden, proj_out, lengths, query_sketch)
+        aligned = proj_hidden.shape[1] % 128 == 0 and proj_hidden.shape[2] == 64
+        if aligned and lengths.shape[0] == 1 and out_grad.shape[1] == LEN and n % 4 == 0 and n >= 8:
+            return fused(n, *args)
+        return plain(*args)
+
     return jax.shard_map(
         on_device,
         mesh=mesh,

time: 96.2 us -> 40.9 us (0.43)
  waiting for transfers between devices: 49.5 us -> 0 us
  Pallas kernels: 0 us -> 34.7 us
  blocking collectives: 20.5 us -> 0 us
  between operations: 14.1 us -> 0.67 us
  matrix products: 11.2 us -> 0 us
  local copies, waits for them, and re-layouts: 0.77 us -> 5.3 us
    all_gather x1 -> x0, waiting for transfers between devices: 48.7 us -> none  [on_device(): lax.all_gather(proj_hidden, 'dp', axis=1, tiled=True)]
    pallas_call x0 -> x1, Pallas kernels: none -> 34.7 us  [fused(): pl.pallas_call(functools.partial(fused_kernel, n), out_shape=jax.ShapeDty...]
    all_gather x1 -> x0, blocking collectives: 20.5 us -> none  [on_device(): lax.all_gather(stacked, 'dp', axis=0, tiled=True)]
    dot_general x6 -> x0, matrix products: 11.2 us -> none  [the longest x1 6.77 us: on_device(): jnp.einsum('lth,lhr->ltr', hidden_in, lax.all_gather(proj_hidden, 'dp', a...]
    unnamed x3 -> x9, local copies, waits for them, and re-layouts: 0.1 us -> 5.3 us
  transfers between devices with their start and end apart: 1 -> 0, of which waited for: 1 -> 0; matrix products, arithmetic and copies ran while one was open for 4% -> 0% of each run, Pallas kernels for 0% -> 0%
where the time goes in v1:
time: 40.9 us; the launch traced here: 40.7 us
  Pallas kernels  34.7 us (85%)
  local copies, waits for them, and re-layouts  5.3 us (13%)
  between operations  0.67 us (2%)
    pallas_call x1, Pallas kernels, fused(): pl.pallas_call(functools.partial(fused_kernel, n), out_shape=jax.ShapeDty...  34.7 us
    unnamed x9, local copies, waits for them, and re-layouts  5.3 us

profile of v1, /device:TPU:0, one launch (start us, length us, event | category | flops | bytes accessed | tf_op | source)
XLA Modules:
  0.0 40.7 jit_solution(11702786834602058250)
XLA Ops:
  0.7 0.0 copy-start
  0.7 1.6 %copy-done = bf16[2,128,4096]{2,1,0:T(8,128)(2,1)S(1)} copy-done((bf16[2,128,4096]{2,1,0:T(8,128)(2,1)S(1)}, bf16[2,128,4096]{2,1,0:T(8,128)(2,1)}, u32[]{:S(2)}) %copy-start) | copy-done | bytes 2097176
  2.2 0.0 copy-start.1
  2.2 1.2 %copy-done.1 = bf16[2,4096,64]{1,2,0:T(8,128)(2,1)S(1)} copy-done((bf16[2,4096,64]{1,2,0:T(8,128)(2,1)S(1)}, bf16[2,4096,64]{1,2,0:T(8,128)(2,1)}, u32[]{:S(2)}) %copy-start.1) | copy-done | bytes 1048600
  3.5 0.0 copy-start.2
  3.5 0.9 %copy-done.2 = bf16[16,8192]{1,0:T(8,128)(2,1)S(1)} copy-done((bf16[16,8192]{1,0:T(8,128)(2,1)S(1)}, bf16[16,8192]{1,0:T(8,128)(2,1)}, u32[]{:S(2)}) %copy-start.2) | copy-done | bytes 262168
  4.4 0.0 copy-start.3
  4.4 0.9 %copy-done.3 = bf16[2,896,64]{1,2,0:T(8,128)(2,1)S(1)} copy-done((bf16[2,896,64]{1,2,0:T(8,128)(2,1)S(1)}, bf16[2,896,64]{1,2,0:T(8,128)(2,1)}, u32[]{:S(2)}) %copy-start.3) | copy-done | bytes 229400
  5.4 34.7 %shard_map.64 = f32[16,16]{1,0:T(8,128)S(1)} custom-call(s32[1]{0:T(128)S(6)} %copy.8.len_ref, bf16[2,128,14336]{2,1,0:T(8,128)(2,1)} %hid_ref.1, bf16[2,128,4096]{2,1,0:T(8,128)(2,1)S(1)} %copy-done, bf16[2,64,896]{2,1,0:T(8,128)(2,1)S(1)} %bitcast.3, bf16[2,64,4096]{2,1,0:T(8,128)(2,1)S(1)} %bitcast.2, bf16[16,8192]{1,0:T(8,128)(2,1)S(1)} %copy-done.2), custom_call_target="tpu_custom_call" | custom-call | flops 603979776 | bytes 9437184 | tf_op jit(solution)/shard_map/pallas_call | solution.py:246
  40.1 0.6 %copy.9 = f32[16,16]{1,0:T(8,128)} copy(f32[16,16]{1,0:T(8,128)S(1)} %shard_map.64) | data formatting | bytes 2048
Async XLA Ops:
  0.7 1.6 %copy-start = (bf16[2,128,4096]{2,1,0:T(8,128)(2,1)S(1)}, bf16[2,128,4096]{2,1,0:T(8,128)(2,1)}, u32[]{:S(2)}) copy-start(bf16[2,128,4096]{2,1,0:T(8,128)(2,1)} %grad_ref.1) | copy-start | bytes 6291460
  2.2 1.2 %copy-start.1 = (bf16[2,4096,64]{1,2,0:T(8,128)(2,1)S(1)}, bf16[2,4096,64]{1,2,0:T(8,128)(2,1)}, u32[]{:S(2)}) copy-start(bf16[2,4096,64]{1,2,0:T(8,128)(2,1)} %param.9) | copy-start | bytes 3145732
  3.5 0.9 %copy-start.2 = (bf16[16,8192]{1,0:T(8,128)(2,1)S(1)}, bf16[16,8192]{1,0:T(8,128)(2,1)}, u32[]{:S(2)}) copy-start(bf16[16,8192]{1,0:T(8,128)(2,1)} %query_ref.1) | copy-start | bytes 786436
  4.4 0.9 %copy-start.3 = (bf16[2,896,64]{1,2,0:T(8,128)(2,1)S(1)}, bf16[2,896,64]{1,2,0:T(8,128)(2,1)}, u32[]{:S(2)}) copy-start(bf16[2,896,64]{1,2,0:T(8,128)(2,1)} %param.8) | copy-start | bytes 688132

commit v2 on v1

--- a/solution.py
+++ b/solution.py
@@ -85,16 +85,14 @@
         return copy
 
     barrier = pltpu.get_barrier_semaphore()
-    for step in range(1, n):
-        pl.semaphore_signal(
-            barrier, inc=1, device_id={"dp": lax.rem(me + step, n)}, device_id_type=MESH
-        )
+    for other in (up, down, pair):
+        pl.semaphore_signal(barrier, inc=1, device_id={"dp": other}, device_id_type=MESH)
     load_grad = load(grad_ref, grad)
     load_pout = load(pout_ref, pout)
     load_own = load(fac_ref, held.at[:, 0, 0])
     load_hid = [load(hid_ref.at[layer], hid.at[layer]) for layer in range(layers)]
     load_query = load(query_ref, query)
-    pl.semaphore_wait(barrier, n - 1)
+    pl.semaphore_wait(barrier, 3)
 
     sent = []
 
@@ -266,7 +264,7 @@
             dma((layers, n)),
         ],
         compiler_params=pltpu.CompilerParams(
-            collective_id=0, has_side_effects=True, vmem_limit_bytes=48 << 20
+            collective_id=0, has_side_effects=True, vmem_limit_bytes=63 << 20
         ),
         cost_estimate=pl.CostEstimate(
             flops=2 * layers * tokens * rank * (hidden + out_grad.shape[2]),

time: 40.9 us -> 36.9 us (0.902)
  local copies, waits for them, and re-layouts: 5.3 us -> 1.3 us
    unnamed x9 -> x1, local copies, waits for them, and re-layouts: 5.3 us -> 1.3 us
where the time goes in v2:
time: 36.9 us; the launch traced here: 36.7 us
  Pallas kernels  34.7 us (94%)
  local copies, waits for them, and re-layouts  1.3 us (4%)
  between operations  0.66 us (2%)
    pallas_call x1, Pallas kernels, fused(): pl.pallas_call(functools.partial(fused_kernel, n), out_shape=jax.ShapeDty...  34.7 us
    unnamed x1, local copies, waits for them, and re-layouts  1.3 us

profile of v2, /device:TPU:0, one launch (start us, length us, event | category | flops | bytes accessed | tf_op | source)
XLA Modules:
  0.0 36.7 jit_solution(1510737712560429924)
XLA Ops:
  0.7 34.7 %shard_map.64 = f32[16,16]{1,0:T(8,128)} custom-call(s32[1]{0:T(128)S(6)} %copy.8.len_ref, bf16[2,128,14336]{2,1,0:T(8,128)(2,1)} %hid_ref.1, bf16[2,128,4096]{2,1,0:T(8,128)(2,1)} %grad_ref.1, bf16[2,64,896]{2,1,0:T(8,128)(2,1)} %bitcast.3, bf16[2,64,4096]{2,1,0:T(8,128)(2,1)} %bitcast.2, bf16[16,8192]{1,0:T(8,128)(2,1)} %query_ref.1), custom_call_target="tpu_custom_call" | custom-call | flops 603979776 | bytes 9437184 | tf_op jit(solution)/shard_map/pallas_call | solution.py:244
  35.4 1.3 %copy.9 = f32[16,16]{1,0:T(8,128)} copy(f32[16,16]{1,0:T(8,128)} %shard_map.64) | data formatting | bytes 2048

commit v3 on v2

--- a/solution.py
+++ b/solution.py
@@ -10,6 +10,7 @@
 
 LEN = 128
 MESH = pl.DeviceIdType.MESH
+RELAYED = (0,)
 ROWS_BY_ROWS = (((1,), (1,)), ((), ()))
 
 
@@ -172,11 +173,11 @@
         ) * (1.0 / math.sqrt(LEN))
         flat = jnp.concatenate([sketch[: rank // 2], sketch[rank // 2 :]], axis=1)
         sketches[layer, me] = flat.astype(jnp.bfloat16)
-        for step in range(1, n):
-            send(
-                sketches.at[layer, me], sketches.at[layer, me],
-                sk_send.at[layer, step], sk_recv.at[layer, step], lax.rem(me + step, n),
-            )
+        mine = sketches.at[layer, me]
+        if layer in RELAYED:
+            send(mine, mine, sk_send.at[layer, 1], sk_recv.at[layer, 1], pair)
+        for step in range(2, n, 2) if layer in RELAYED else range(1, n):
+            send(mine, mine, sk_send.at[layer, step], sk_recv.at[layer, step], lax.rem(me + step, n))
 
     for layer in range(layers):
         load_hid[layer].wait()
@@ -211,16 +212,29 @@
                 add(layer, 1, half)
                 finish(layer)
 
+    def sketch_arrived(layer, step, source):
+        ref = sketches.at[layer, lax.rem(source, n)]
+        pltpu.make_async_remote_copy(
+            src_ref=ref, dst_ref=ref, send_sem=sk_send.at[layer, step], recv_sem=sk_recv.at[layer, step],
+            device_id={"dp": pair}, device_id_type=MESH,
+        ).wait_recv()
+        return ref
+
+    for layer in RELAYED:
+        for step in range(2, n, 2):
+            ref = sketch_arrived(layer, step, me + n - step)
+            send(ref, ref, sk_send.at[layer, step + 1], sk_recv.at[layer, step + 1], pair)
+
     load_query.wait()
     scores = jnp.zeros((query.shape[0], n), jnp.float32)
     width = rank * rank
     for layer in range(layers):
-        for step in range(1, n):
-            ref = sketches.at[layer, lax.rem(me + n - step, n)]
-            pltpu.make_async_remote_copy(
-                src_ref=ref, dst_ref=ref, send_sem=sk_send.at[layer, step], recv_sem=sk_recv.at[layer, step],
-                device_id={"dp": pair}, device_id_type=MESH,
-            ).wait_recv()
+        if layer in RELAYED:
+            for step in range(0, n, 2):
+                sketch_arrived(layer, step + 1, pair + n - step)
+        else:
+            for step in range(1, n):
+                sketch_arrived(layer, step, me + n - step)
         lines = width // 128
         spread[...] = sketches[layer].astype(jnp.float32).reshape(n * lines, 128)
         flat = jnp.concatenate(

time: 36.9 us -> 35.7 us (0.967)
  Pallas kernels: 34.7 us -> 33.6 us
    pallas_call x1, Pallas kernels: 34.7 us -> 33.6 us  [fused(): pl.pallas_call(functools.partial(fused_kernel, n), out_shape=jax.ShapeDty...]
where the time goes in v3:
time: 35.7 us; the launch traced here: 35.5 us
  Pallas kernels  33.6 us (94%)
  local copies, waits for them, and re-layouts  1.3 us (4%)
  between operations  0.66 us (2%)
    pallas_call x1, Pallas kernels, fused(): pl.pallas_call(functools.partial(fused_kernel, n), out_shape=jax.ShapeDty...  33.6 us
    unnamed x1, local copies, waits for them, and re-layouts  1.3 us

profile of v3, /device:TPU:0, one launch (start us, length us, event | category | flops | bytes accessed | tf_op | source)
XLA Modules:
  0.0 35.5 jit_solution(8447113164121825090)
XLA Ops:
  0.7 33.6 %shard_map.64 = f32[16,16]{1,0:T(8,128)} custom-call(s32[1]{0:T(128)S(6)} %copy.8.len_ref, bf16[2,128,14336]{2,1,0:T(8,128)(2,1)} %hid_ref.1, bf16[2,128,4096]{2,1,0:T(8,128)(2,1)} %grad_ref.1, bf16[2,64,896]{2,1,0:T(8,128)(2,1)} %bitcast.3, bf16[2,64,4096]{2,1,0:T(8,128)(2,1)} %bitcast.2, bf16[16,8192]{1,0:T(8,128)(2,1)} %query_ref.1), custom_call_target="tpu_custom_call" | custom-call | flops 603979776 | bytes 9437184 | tf_op jit(solution)/shard_map/pallas_call | solution.py:258
  34.2 1.3 %copy.9 = f32[16,16]{1,0:T(8,128)} copy(f32[16,16]{1,0:T(8,128)} %shard_map.64) | data formatting | bytes 2048

commit v4 on v3

--- a/solution.py
+++ b/solution.py
@@ -88,9 +88,9 @@
     barrier = pltpu.get_barrier_semaphore()
     for other in (up, down, pair):
         pl.semaphore_signal(barrier, inc=1, device_id={"dp": other}, device_id_type=MESH)
+    load_own = load(fac_ref, held.at[:, 0, 0])
     load_grad = load(grad_ref, grad)
     load_pout = load(pout_ref, pout)
-    load_own = load(fac_ref, held.at[:, 0, 0])
     load_hid = [load(hid_ref.at[layer], hid.at[layer]) for layer in range(layers)]
     load_query = load(query_ref, query)
     pl.semaphore_wait(barrier, 3)
@@ -204,8 +204,14 @@
                 add(layer, 1, 0)
             else:
                 for slot in (hop - 1, chips - hop + 1):
-                    arrived(layer, 1, slot)
-                    add(layer, 1, slot)
+                    if hop < half or layer:
+                        arrived(layer, 1, slot)
+                        add(layer, 1, slot)
+            if hop == half - 1 and layer == layers - 1:
+                for early in range(layers - 1):
+                    for slot in (hop, chips - hop):
+                        arrived(early, 1, slot)
+                        add(early, 1, slot)
             if hop == half:
                 arrived(layer, 1, half)
                 arrived(layer, 1, chips)
@@ -225,6 +231,9 @@
             ref = sketch_arrived(layer, step, me + n - step)
             send(ref, ref, sk_send.at[layer, step + 1], sk_recv.at[layer, step + 1], pair)
 
+    last = len(sent) - (n - 1) - (n // 2 - 1)
+    for copy in sent[:last]:
+        copy.wait_send()
     load_query.wait()
     scores = jnp.zeros((query.shape[0], n), jnp.float32)
     width = rank * rank
@@ -244,7 +253,7 @@
             query[:, layer * width : (layer + 1) * width], flat, ROWS_BY_ROWS, preferred_element_type=jnp.float32
         )
     out_ref[...] = scores * (1.0 / math.sqrt(layers * width))
-    for copy in sent:
+    for copy in sent[last:]:
         copy.wait_send()
 
 

time: 35.7 us -> 35.6 us (level)
  no operation moved by 1% of the time
where the time goes in v4:
time: 35.6 us; the launch traced here: 35.4 us
  Pallas kernels  33.4 us (94%)
  local copies, waits for them, and re-layouts  1.3 us (4%)
  between operations  0.66 us (2%)
    pallas_call x1, Pallas kernels, fused(): pl.pallas_call(functools.partial(fused_kernel, n), out_shape=jax.ShapeDty...  33.4 us
    unnamed x1, local copies, waits for them, and re-layouts  1.3 us

profile of v4, /device:TPU:0, one launch (start us, length us, event | category | flops | bytes accessed | tf_op | source)
XLA Modules:
  0.0 35.4 jit_solution(12878915795711807444)
XLA Ops:
  0.7 33.4 %shard_map.64 = f32[16,16]{1,0:T(8,128)} custom-call(s32[1]{0:T(128)S(6)} %copy.8.len_ref, bf16[2,128,14336]{2,1,0:T(8,128)(2,1)} %hid_ref.1, bf16[2,128,4096]{2,1,0:T(8,128)(2,1)} %grad_ref.1, bf16[2,64,896]{2,1,0:T(8,128)(2,1)} %bitcast.3, bf16[2,64,4096]{2,1,0:T(8,128)(2,1)} %bitcast.2, bf16[16,8192]{1,0:T(8,128)(2,1)} %query_ref.1), custom_call_target="tpu_custom_call" | custom-call | flops 603979776 | bytes 9437184 | tf_op jit(solution)/shard_map/pallas_call | solution.py:267
  34.1 1.3 %copy.9 = f32[16,16]{1,0:T(8,128)} copy(f32[16,16]{1,0:T(8,128)} %shard_map.64) | data formatting | bytes 2048
